TPU v7x, 1024 devices: a whole 4x4x32 slice. The times are simulated.
1024 devices in a mesh: dp: 128 (over z, x), tensor: 8 (over y, core).
Axes of the slice: x: 4, y: 4, z: 32, core: 2. Of those that a mesh axis runs over, the one named last changes fastest.
Arguments:
- activations: bfloat16 [65536, 8192], P('dp', 'tensor'), may hold values from -6 to 6
- output_gradient: bfloat16 [65536, 1024], P(('dp', 'tensor')), may hold values from -0.25 to 0.25
- momentum: bfloat16 [128, 8192, 1024], P('dp', 'tensor'), may hold values from -6 to 6
Outputs:
- update: bfloat16 [8192, 1024], P('tensor')
All inputs are finite; a program needn't handle non-finite values.
Results may differ from a plain program's by a relative error of at most 0.0051.
Values may be sent and summed in bfloat16 or wider, within the bound.
A program may use at most 64 MiB of HBM per device.

v0:
```python
import functools

import jax
import jax.numpy as jnp
import numpy as np
from jax import lax
from jax.experimental import pallas as pl
from jax.experimental.pallas import tpu as pltpu
from jax.sharding import PartitionSpec as P
import ml_dtypes

BLOCK_SIDE = 64
KEPT_FREQUENCY = 8
MESH = pl.DeviceIdType.MESH
F32 = jnp.float32
BF16 = jnp.bfloat16

ROWS = 1024
COLS = 1024
TOKENS = 512
KEPT = ROWS // BLOCK_SIDE * KEPT_FREQUENCY
TENSOR = 8
SHARE = TOKENS // TENSOR
GROUP = 16
OWNERS = 8
STRIP = KEPT // OWNERS
SQUARES = 8
FAR = SQUARES // 2
ORDER = (0, 1, 2, 7, 6, 3, 5)
LEVELS = (4, 2)


def block_basis():
    freq = np.arange(KEPT_FREQUENCY)[:, None]
    place = np.arange(BLOCK_SIDE)[None, :]
    scales = np.where(freq == 0, np.sqrt(1.0 / BLOCK_SIDE), np.sqrt(2.0 / BLOCK_SIDE))
    basis = scales * np.cos(np.pi * (2.0 * place + 1.0) * freq / (2.0 * BLOCK_SIDE))
    return np.kron(np.eye(ROWS // BLOCK_SIDE), basis).astype(np.float32)


def two_parts(value, axis):
    high = value.astype(BF16)
    low = (value - high.astype(F32)).astype(BF16)
    return jnp.concatenate([high, low], axis=axis)


def fold_rows(value):
    half = value.shape[0] // 2
    return value[:half] + value[half:]


def fold_cols(value):
    half = value.shape[1] // 2
    return value[:, :half] + value[:, half:]


def dot(a, b):
    return jnp.dot(a, b, preferred_element_type=F32)


def dot_nt(a, b):
    return lax.dot_general(a, b, (((1,), (1,)), ((), ())), preferred_element_type=F32)


def step_kernel(
    acts_hbm, grad_hbm, moment_hbm, wide_hbm, tall_hbm, summed_ref, wide,
    acts, grad, moment, wide_full, tall_full, tall, gathered, coeffs, strips, partials, table, total,
    load_sem, gather_send, gather_recv, strip_send, strip_recv,
    first_send, across_send, partial_recv, table_send, table_recv, known,
):
    dp, tensor = lax.axis_index("dp"), lax.axis_index("tensor")
    square, place = dp // GROUP, lax.rem(dp, GROUP)
    core = lax.rem(tensor, 2)

    is_owner = core == 1
    own_table = place >= OWNERS
    held = jnp.where(own_table, tensor, tensor - 1)
    held_strip = lax.rem(place, OWNERS)

    def peer(step):
        return (dp, lax.rem(tensor + step, TENSOR))

    def mate(step):
        return (square * GROUP + lax.rem(place + step, GROUP), tensor)

    def across_cores(step):
        return (square * GROUP + lax.rem(place + step, GROUP), tensor + 1 - 2 * core)

    def ahead(step):
        return (lax.rem(square + step, SQUARES) * GROUP + place, tensor)

    barrier = pltpu.get_barrier_semaphore()
    greeted = [ahead(1), ahead(SQUARES - 1)]
    greeted += [mate(step) for step in range(1, GROUP)]
    greeted += [across_cores(step) for step in range(1, GROUP)]
    greeted += [peer(step) for step in range(1, TENSOR)]
    for device in greeted:
        pl.semaphore_signal(barrier, inc=1, device_id=device, device_id_type=MESH)

    loads = [
        pltpu.make_async_copy(source, target, load_sem.at[i])
        for i, (source, target) in enumerate(
            [(grad_hbm, grad), (tall_hbm, tall_full), (wide_hbm, wide_full), (acts_hbm, acts)]
            + [
                (moment_hbm.at[0, pl.ds(256 * i, 256)], moment.at[pl.ds(256 * i, 256)])
                for i in range(4)
            ]
        )
    ]
    for load in loads:
        load.start()

    loads[0].wait()
    loads[1].wait()
    tall[...] = two_parts(tall_full[...], 1)
    mine = pl.ds(pl.multiple_of(tensor * SHARE, SHARE), SHARE)
    gathered[mine] = fold_cols(dot(grad[...], tall[...])).astype(BF16)
    pl.semaphore_wait(barrier, len(greeted))
    gathers = []
    for step in (4, 3, 5, 2, 6, 7, 1):
        copy = pltpu.make_async_remote_copy(
            src_ref=gathered.at[mine],
            dst_ref=gathered.at[mine],
            send_sem=gather_send.at[step],
            recv_sem=gather_recv.at[step],
            device_id=peer(step),
            device_id_type=MESH,
        )
        copy.start()
        gathers.append(copy)

    def pass_on(way, level):
        if level > 0:
            pl.semaphore_wait(known.at[way, level - 1], 1)
        if level < LEVELS[way]:
            target = ahead(1) if way == 0 else ahead(SQUARES - 1)
            pl.semaphore_signal(known.at[way, level], inc=1, device_id=target, device_id_type=MESH)

    pass_on(0, 0)
    pass_on(1, 0)

    loads[2].wait()
    wide[...] = two_parts(wide_full[...], 0)
    loads[3].wait()
    rows = two_parts(fold_rows(dot_nt(wide[...], acts[...])), 0)
    kept = jnp.zeros((2 * KEPT, 2 * KEPT), F32)
    for i in range(4):
        loads[4 + i].wait()
        part = slice(256 * i, 256 * (i + 1))
        half = two_parts(fold_cols(dot(moment[part], tall[...])), 1)
        kept += dot(wide[:, part], half)
    kept = 0.9 * fold_cols(fold_rows(kept))

    pass_on(0, 1)
    pass_on(1, 1)

    for copy in gathers:
        copy.wait_recv()
    found = fold_rows(dot(rows, gathered[...])) + kept
    coeffs[...] = found.reshape(OWNERS, STRIP, KEPT).astype(BF16)

    def to_owner(turn):
        strip = 4 * (turn % 2) + lax.rem(place + (2, 1, 3, 0)[turn // 2], 4)
        owner = strip + OWNERS * core
        return jnp.logical_or(core == 0, owner != place), pltpu.make_async_remote_copy(
            src_ref=coeffs.at[strip],
            dst_ref=strips.at[place],
            send_sem=strip_send.at[turn],
            recv_sem=strip_recv.at[place],
            device_id=(square * GROUP + owner, tensor + 1 - core),
            device_id_type=MESH,
        )

    for turn in range(OWNERS):
        other, copy = to_owner(turn)
        pl.when(other)(copy.start)
    pass_on(0, 2)
    pass_on(1, 2)
    pass_on(0, 3)

    def to_first(mate):
        return pltpu.make_async_remote_copy(
            src_ref=partials.at[square, held_strip],
            dst_ref=partials.at[square, held_strip],
            send_sem=first_send.at[mate],
            recv_sem=partial_recv.at[square, held_strip],
            device_id=(mate, held),
            device_id_type=MESH,
        )

    def across(step):
        return jnp.logical_or(square != FAR, step != SQUARES - FAR), pltpu.make_async_remote_copy(
            src_ref=partials.at[square, held_strip],
            dst_ref=partials.at[square, held_strip],
            send_sem=across_send.at[step],
            recv_sem=partial_recv.at[square, held_strip],
            device_id=ahead(step),
            device_id_type=MESH,
        )

    def to_mate(turn):
        mate = turn // 4 * 4 + lax.rem(place + (2, 1, 3, 0)[turn % 4], 4)
        elsewhere = jnp.logical_or(jnp.logical_not(own_table), mate != place)
        return elsewhere, pltpu.make_async_remote_copy(
            src_ref=total,
            dst_ref=table.at[held_strip],
            send_sem=table_send.at[turn],
            recv_sem=table_recv.at[held_strip],
            device_id=(square * GROUP + mate, held),
            device_id_type=MESH,
        )

    def wait_strip(source):
        pltpu.make_async_copy(strips.at[source], strips.at[source], strip_recv.at[source]).wait()

    def wait_partial(source, strip):
        piece = partials.at[source, strip]
        pltpu.make_async_copy(piece, piece, partial_recv.at[source, strip]).wait()

    @pl.when(is_owner)
    def _():
        for step in range(1, GROUP):
            wait_strip(lax.rem(place + step, GROUP))

        @pl.when(own_table)
        def _():
            strips[place] = coeffs[held_strip]

        pl.when(jnp.logical_not(own_table))(functools.partial(wait_strip, place))
        partials[square, held_strip] = jnp.sum(strips[...].astype(F32), axis=0).astype(BF16)

    @pl.when(square == FAR)
    def _():
        pass_on(0, 4)

    @pl.when(jnp.logical_and(square == FAR, is_owner))
    def _():
        for mate in range(GROUP):
            to_first(mate).start()

    @pl.when(is_owner)
    def _():
        for step in (4, 3, 5, 2, 6, 1, 7):
            other, copy = across(step)
            pl.when(other)(copy.start)

    @pl.when(square != FAR)
    def _():
        pass_on(0, 4)

    for copy in gathers:
        copy.wait_send()
    for turn in range(OWNERS):
        other, copy = to_owner(turn)
        pl.when(other)(copy.wait_send)

    @pl.when(is_owner)
    def _():
        for step in (1, 7, 2, 6, 3, 5, 4):
            source = lax.rem(square + step, SQUARES)
            if step == FAR:
                pl.when(square != 0)(functools.partial(wait_partial, source, held_strip))
            else:
                wait_partial(source, held_strip)
        added = partials[0, held_strip].astype(F32)
        for source in ORDER[1:]:
            added += partials[source, held_strip].astype(F32)
        total[...] = added

        @pl.when(square != 0)
        def _():
            total[...] += partials[FAR, held_strip].astype(F32)

        for turn in range(GROUP):
            other, copy = to_mate(turn)
            pl.when(other)(copy.start)

        @pl.when(own_table)
        def _():
            pltpu.make_async_copy(total, table.at[held_strip], table_recv.at[held_strip]).start()

    for strip in range(OWNERS):
        pltpu.make_async_copy(total, table.at[strip], table_recv.at[strip]).wait()

    @pl.when(square == 0)
    def _():
        for strip in range(OWNERS):
            wait_partial(FAR, strip)
        summed_ref[...] = (table[...] + partials[FAR].astype(F32)).reshape(KEPT, KEPT)

    @pl.when(square != 0)
    def _():
        summed_ref[...] = table[...].reshape(KEPT, KEPT)

    @pl.when(is_owner)
    def _():
        for step in range(1, SQUARES):
            other, copy = across(step)
            pl.when(other)(copy.wait_send)
        for turn in range(GROUP):
            other, copy = to_mate(turn)
            pl.when(other)(copy.wait_send)

    @pl.when(jnp.logical_and(square == FAR, is_owner))
    def _():
        for mate in range(GROUP):
            to_first(mate).wait_send()


def expand_kernel(summed_ref, wide, block_ref, out_hbm, out, out_sem):
    summed = two_parts(summed_ref[...], 0)
    half = fold_rows(dot(summed, wide[:KEPT])) + dot(summed[:KEPT], wide[KEPT:])
    half = two_parts(half, 0)
    square_basis = block_ref[...].astype(BF16)
    copies = []
    for i in range(4):
        high = half[32 * i : 32 * (i + 1)]
        low = half[KEPT + 32 * i : KEPT + 32 * (i + 1)]
        out[i] = dot(square_basis, jnp.concatenate([high, high, low], axis=0)).astype(BF16)
        copy = pltpu.make_async_copy(out.at[i], out_hbm.at[pl.ds(256 * i, 256)], out_sem.at[i])
        copy.start()
        copies.append(copy)
    for copy in copies:
        copy.wait()


def per_device(activations, output_gradient, momentum):
    wide = block_basis()
    corner = wide[:32, :256].T
    high = corner.astype(ml_dtypes.bfloat16).astype(np.float32)
    block = np.concatenate([high, corner - high, high], axis=1)
    wide, tall, block = jnp.asarray(wide), jnp.asarray(wide.T.copy()), jnp.asarray(block)
    anywhere = pl.BlockSpec(memory_space=pl.ANY)
    in_vmem = pl.BlockSpec(memory_space=pltpu.VMEM)
    dma = pltpu.SemaphoreType.DMA
    operands = (activations, output_gradient, momentum, wide, tall)
    summed, wide = pl.pallas_call(
        step_kernel,
        out_shape=(pltpu.VMEM((KEPT, KEPT), F32), pltpu.VMEM((2 * KEPT, ROWS), BF16)),
        in_specs=[anywhere] * 5,
        out_specs=(in_vmem, in_vmem),
        scratch_shapes=[
            pltpu.VMEM((TOKENS, ROWS), BF16),
            pltpu.VMEM((SHARE, COLS), BF16),
            pltpu.VMEM((ROWS, COLS), BF16),
            pltpu.VMEM((KEPT, ROWS), F32),
            pltpu.VMEM((ROWS, KEPT), F32),
            pltpu.VMEM((ROWS, 2 * KEPT), BF16),
            pltpu.VMEM((TOKENS, KEPT), BF16),
            pltpu.VMEM((OWNERS, STRIP, KEPT), BF16),
            pltpu.VMEM((GROUP, STRIP, KEPT), BF16),
            pltpu.VMEM((SQUARES, OWNERS, STRIP, KEPT), BF16),
            pltpu.VMEM((OWNERS, STRIP, KEPT), F32),
            pltpu.VMEM((STRIP, KEPT), F32),
            dma((8,)),
            dma((TENSOR,)),
            dma((TENSOR,)),
            dma((OWNERS,)),
            dma((GROUP,)),
            dma((GROUP,)),
            dma((SQUARES,)),
            dma((SQUARES, OWNERS)),
            dma((GROUP,)),
            dma((OWNERS,)),
            pltpu.SemaphoreType.REGULAR((2, 4)),
        ],
        compiler_params=pltpu.CompilerParams(
            collective_id=0, has_side_effects=True, vmem_limit_bytes=24 * 2**20
        ),
        name="step",
    )(*[pltpu.with_memory_space_constraint(value, pltpu.HBM) for value in operands])
    return pl.pallas_call(
        expand_kernel,
        out_shape=jax.ShapeDtypeStruct((ROWS, COLS), BF16),
        in_specs=[in_vmem] * 3,
        out_specs=anywhere,
        scratch_shapes=[pltpu.VMEM((4, 256, COLS), BF16), dma((4,))],
        compiler_params=pltpu.CompilerParams(vmem_limit_bytes=24 * 2**20),
        name="expand",
    )(summed, wide, block)


def solution(mesh):
    return jax.shard_map(
        per_device,
        mesh=mesh,
        in_specs=(P("dp", "tensor"), P(("dp", "tensor"), None), P("dp", "tensor", None)),
        out_specs=P("tensor", None),
        check_vma=False,
    )
```

profile of v0, /device:TPU:1, one launch (start us, length us, event | category | flops | bytes accessed | tf_op | source)
XLA Modules:
  0.0 48.5 jit_solution(2902040086329489177)
XLA Ops:
  0.0 0.0 copy-start
  0.0 46.6 %step.1 = (f32[128,128]{1,0:T(8,128)S(1)}, bf16[256,1024]{1,0:T(8,128)(2,1)S(1)}) custom-call(bf16[512,1024]{1,0:T(8,128)(2,1)} %acts_hbm.1, bf16[64,1024]{1,0:T(8,128)(2,1)} %grad_hbm.1, bf16[1,1024,1024]{2,1,0:T(8,128)(2,1)} %moment_hbm.1, f32[128,1024]{1,0:T(8,128)} %constant.6.clone.wide_hbm, f32[1024,128]{1,0:T(8,128)} %constant.7.clone.tall_hbm), custom_call_target="tpu_custom_call" | custom-call | tf_op jit(solution)/shard_map/step/pallas_call | solution.py:337
  46.6 0.0 copy-done
  46.6 1.9 %expand.1 = bf16[1024,1024]{1,0:T(8,128)(2,1)} custom-call(f32[128,128]{1,0:T(8,128)S(1)} %get-tuple-element.7.summed_ref, bf16[256,1024]{1,0:T(8,128)(2,1)S(1)} %get-tuple-element.8.wide, f32[256,96]{1,0:T(8,128)S(1)} %copy-done), custom_call_target="tpu_custom_call" | custom-call | tf_op jit(solution)/shard_map/expand/pallas_call | solution.py:372
Async XLA Ops:
  0.0 46.6 %copy-start = (f32[256,96]{1,0:T(8,128)S(1)}, f32[256,96]{1,0:T(8,128)}, u32[]{:S(2)}) copy-start(f32[256,96]{1,0:T(8,128)} %constant.8.clone.block_ref) | copy-start | bytes 294916
where the time goes:
time: 48.7 us; the launch traced here: 48.5 us
  Pallas kernels  48.5 us (100%)
    pallas_call x1, Pallas kernels, per_device(): pl.pallas_call(step_kernel, out_shape=(pltpu.VMEM((KEPT, KEPT), F32), plt...  46.6 us
    pallas_call x1, Pallas kernels, per_device(): pl.pallas_call(expand_kernel, out_shape=jax.ShapeDtypeStruct((ROWS, COLS)...  1.92 us

commit v1 on v0

--- a/solution.py
+++ b/solution.py
@@ -26,8 +26,9 @@
 STRIP = KEPT // OWNERS
 SQUARES = 8
 FAR = SQUARES // 2
-ORDER = (0, 1, 2, 7, 6, 3, 5)
-LEVELS = (4, 2)
+ORDER = (0, 1, 2, 7, 6)
+LAST = (3, 5, FAR)
+LEVELS = (4, 3)
 
 
 def block_basis():
@@ -64,13 +65,14 @@
 
 def step_kernel(
     acts_hbm, grad_hbm, moment_hbm, wide_hbm, tall_hbm, summed_ref, wide,
-    acts, grad, moment, wide_full, tall_full, tall, gathered, coeffs, strips, partials, table, total,
+    acts, grad, moment, wide_full, tall_full, tall, rows, gathered, coeffs, strips, partials, table, total,
     load_sem, gather_send, gather_recv, strip_send, strip_recv,
     first_send, across_send, partial_recv, table_send, table_recv, known,
 ):
     dp, tensor = lax.axis_index("dp"), lax.axis_index("tensor")
     square, place = dp // GROUP, lax.rem(dp, GROUP)
     core = lax.rem(tensor, 2)
+    is_far = jnp.logical_and(square >= FAR - 1, square <= FAR + 1)
 
     is_owner = core == 1
     own_table = place >= OWNERS
@@ -117,7 +119,7 @@
     gathered[mine] = fold_cols(dot(grad[...], tall[...])).astype(BF16)
     pl.semaphore_wait(barrier, len(greeted))
     gathers = []
-    for step in (4, 3, 5, 2, 6, 7, 1):
+    for step in (4, 5 - 2 * core, 3 + 2 * core, 2, 6, 7, 1):
         copy = pltpu.make_async_remote_copy(
             src_ref=gathered.at[mine],
             dst_ref=gathered.at[mine],
@@ -142,7 +144,7 @@
     loads[2].wait()
     wide[...] = two_parts(wide_full[...], 0)
     loads[3].wait()
-    rows = two_parts(fold_rows(dot_nt(wide[...], acts[...])), 0)
+    rows[...] = two_parts(fold_rows(dot_nt(wide[...], acts[...])), 0)
     kept = jnp.zeros((2 * KEPT, 2 * KEPT), F32)
     for i in range(4):
         loads[4 + i].wait()
@@ -154,9 +156,20 @@
     pass_on(0, 1)
     pass_on(1, 1)
 
-    for copy in gathers:
-        copy.wait_recv()
-    found = fold_rows(dot(rows, gathered[...])) + kept
+    def of_chip(step):
+        spot = lax.rem(tensor // 2 + step, TENSOR // 2) * 2 * SHARE
+        tokens = pl.ds(pl.multiple_of(spot, 2 * SHARE), 2 * SHARE)
+        return dot(rows[:, tokens], gathered[tokens])
+
+    def wait_tokens(step):
+        pltpu.make_async_copy(gathered.at[mine], gathered.at[mine], gather_recv.at[step]).wait()
+
+    for step in (1, 2, 6, 7, 5 - 2 * core):
+        wait_tokens(step)
+    found = of_chip(0) + of_chip(1) + of_chip(3)
+    for step in (4, 3 + 2 * core):
+        wait_tokens(step)
+    found = fold_rows(found + of_chip(2)) + kept
     coeffs[...] = found.reshape(OWNERS, STRIP, KEPT).astype(BF16)
 
     def to_owner(turn):
@@ -189,7 +202,7 @@
         )
 
     def across(step):
-        return jnp.logical_or(square != FAR, step != SQUARES - FAR), pltpu.make_async_remote_copy(
+        return jnp.logical_or(jnp.logical_not(is_far), square + step != SQUARES), pltpu.make_async_remote_copy(
             src_ref=partials.at[square, held_strip],
             dst_ref=partials.at[square, held_strip],
             send_sem=across_send.at[step],
@@ -233,7 +246,11 @@
     def _():
         pass_on(0, 4)
 
-    @pl.when(jnp.logical_and(square == FAR, is_owner))
+    @pl.when(square == FAR + 1)
+    def _():
+        pass_on(1, 3)
+
+    @pl.when(jnp.logical_and(is_far, is_owner))
     def _():
         for mate in range(GROUP):
             to_first(mate).start()
@@ -247,6 +264,10 @@
     @pl.when(square != FAR)
     def _():
         pass_on(0, 4)
+
+    @pl.when(square != FAR + 1)
+    def _():
+        pass_on(1, 3)
 
     for copy in gathers:
         copy.wait_send()
@@ -258,7 +279,7 @@
     def _():
         for step in (1, 7, 2, 6, 3, 5, 4):
             source = lax.rem(square + step, SQUARES)
-            if step == FAR:
+            if step in LAST:
                 pl.when(square != 0)(functools.partial(wait_partial, source, held_strip))
             else:
                 wait_partial(source, held_strip)
@@ -269,7 +290,10 @@
 
         @pl.when(square != 0)
         def _():
-            total[...] += partials[FAR, held_strip].astype(F32)
+            added = total[...]
+            for source in LAST:
+                added += partials[source, held_strip].astype(F32)
+            total[...] = added
 
         for turn in range(GROUP):
             other, copy = to_mate(turn)
@@ -284,9 +308,12 @@
 
     @pl.when(square == 0)
     def _():
-        for strip in range(OWNERS):
-            wait_partial(FAR, strip)
-        summed_ref[...] = (table[...] + partials[FAR].astype(F32)).reshape(KEPT, KEPT)
+        added = table[...]
+        for source in LAST:
+            for strip in range(OWNERS):
+                wait_partial(source, strip)
+            added += partials[source].astype(F32)
+        summed_ref[...] = added.reshape(KEPT, KEPT)
 
     @pl.when(square != 0)
     def _():
@@ -301,7 +328,7 @@
             other, copy = to_mate(turn)
             pl.when(other)(copy.wait_send)
 
-    @pl.when(jnp.logical_and(square == FAR, is_owner))
+    @pl.when(jnp.logical_and(is_far, is_owner))
     def _():
         for mate in range(GROUP):
             to_first(mate).wait_send()
@@ -346,6 +373,7 @@
             pltpu.VMEM((KEPT, ROWS), F32),
             pltpu.VMEM((ROWS, KEPT), F32),
             pltpu.VMEM((ROWS, 2 * KEPT), BF16),
+            pltpu.VMEM((2 * KEPT, TOKENS), BF16),
             pltpu.VMEM((TOKENS, KEPT), BF16),
             pltpu.VMEM((OWNERS, STRIP, KEPT), BF16),
             pltpu.VMEM((GROUP, STRIP, KEPT), BF16),

time: 48.7 us -> 47.9 us (0.984)
  Pallas kernels: 48.5 us -> 47.5 us
    pallas_call x1, Pallas kernels: 46.6 us -> 45.6 us  [per_device(): pl.pallas_call(step_kernel, out_shape=(pltpu.VMEM((KEPT, KEPT), F32), plt...]
where the time goes in v1:
time: 47.9 us; the launch traced here: 47.6 us
  Pallas kernels  47.5 us (99%)
    pallas_call x1, Pallas kernels, per_device(): pl.pallas_call(step_kernel, out_shape=(pltpu.VMEM((KEPT, KEPT), F32), plt...  45.6 us
    pallas_call x1, Pallas kernels, per_device(): pl.pallas_call(expand_kernel, out_shape=jax.ShapeDtypeStruct((ROWS, COLS)...  1.92 us

profile of v1, /device:TPU:1, one launch (start us, length us, event | category | flops | bytes accessed | tf_op | source)
XLA Modules:
  0.0 47.6 jit_solution(13320820195058401911)
XLA Ops:
  0.0 0.0 copy-start
  0.0 45.6 %step.1 = (f32[128,128]{1,0:T(8,128)S(1)}, bf16[256,1024]{1,0:T(8,128)(2,1)S(1)}) custom-call(bf16[512,1024]{1,0:T(8,128)(2,1)} %acts_hbm.1, bf16[64,1024]{1,0:T(8,128)(2,1)} %grad_hbm.1, bf16[1,1024,1024]{2,1,0:T(8,128)(2,1)} %moment_hbm.1, f32[128,1024]{1,0:T(8,128)} %constant.6.clone.wide_hbm, f32[1024,128]{1,0:T(8,128)} %constant.7.clone.tall_hbm), custom_call_target="tpu_custom_call" | custom-call | tf_op jit(solution)/shard_map/step/pallas_call | solution.py:364
  45.6 0.0 copy-done
  45.7 1.9 %expand.1 = bf16[1024,1024]{1,0:T(8,128)(2,1)} custom-call(f32[128,128]{1,0:T(8,128)S(1)} %get-tuple-element.7.summed_ref, bf16[256,1024]{1,0:T(8,128)(2,1)S(1)} %get-tuple-element.8.wide, f32[256,96]{1,0:T(8,128)S(1)} %copy-done), custom_call_target="tpu_custom_call" | custom-call | tf_op jit(solution)/shard_map/expand/pallas_call | solution.py:400
Async XLA Ops:
  0.0 45.6 %copy-start = (f32[256,96]{1,0:T(8,128)S(1)}, f32[256,96]{1,0:T(8,128)}, u32[]{:S(2)}) copy-start(f32[256,96]{1,0:T(8,128)} %constant.8.clone.block_ref) | copy-start | bytes 294916

commit v2 on v1

--- a/solution.py
+++ b/solution.py
@@ -28,7 +28,7 @@
 FAR = SQUARES // 2
 ORDER = (0, 1, 2, 7, 6)
 LAST = (3, 5, FAR)
-LEVELS = (4, 3)
+LEVELS = (3, 3)
 
 
 def block_basis():
@@ -99,6 +99,15 @@
     for device in greeted:
         pl.semaphore_signal(barrier, inc=1, device_id=device, device_id_type=MESH)
 
+    @pl.when(square == 0)
+    def _():
+        for step in range(GROUP):
+            spot = GROUP + lax.rem(place + step, GROUP)
+            for other in (tensor, tensor + 1 - 2 * core)[1 if step == 0 else 0 :]:
+                pl.semaphore_signal(
+                    barrier, inc=1, device_id=(spot, other), device_id_type=MESH
+                )
+
     loads = [
         pltpu.make_async_copy(source, target, load_sem.at[i])
         for i, (source, target) in enumerate(
@@ -117,7 +126,7 @@
     tall[...] = two_parts(tall_full[...], 1)
     mine = pl.ds(pl.multiple_of(tensor * SHARE, SHARE), SHARE)
     gathered[mine] = fold_cols(dot(grad[...], tall[...])).astype(BF16)
-    pl.semaphore_wait(barrier, len(greeted))
+    pl.semaphore_wait(barrier, len(greeted) + jnp.where(square == 1, 2 * GROUP - 1, 0))
     gathers = []
     for step in (4, 5 - 2 * core, 3 + 2 * core, 2, 6, 7, 1):
         copy = pltpu.make_async_remote_copy(
@@ -242,10 +251,6 @@
         pl.when(jnp.logical_not(own_table))(functools.partial(wait_strip, place))
         partials[square, held_strip] = jnp.sum(strips[...].astype(F32), axis=0).astype(BF16)
 
-    @pl.when(square == FAR)
-    def _():
-        pass_on(0, 4)
-
     @pl.when(square == FAR + 1)
     def _():
         pass_on(1, 3)
@@ -260,10 +265,6 @@
         for step in (4, 3, 5, 2, 6, 1, 7):
             other, copy = across(step)
             pl.when(other)(copy.start)
-
-    @pl.when(square != FAR)
-    def _():
-        pass_on(0, 4)
 
     @pl.when(square != FAR + 1)
     def _():
@@ -306,6 +307,15 @@
     for strip in range(OWNERS):
         pltpu.make_async_copy(total, table.at[strip], table_recv.at[strip]).wait()
 
+    @pl.when(is_owner)
+    def _():
+        for step in range(1, SQUARES):
+            other, copy = across(step)
+            pl.when(other)(copy.wait_send)
+        for turn in range(GROUP):
+            other, copy = to_mate(turn)
+            pl.when(other)(copy.wait_send)
+
     @pl.when(square == 0)
     def _():
         added = table[...]
@@ -318,15 +328,6 @@
     @pl.when(square != 0)
     def _():
         summed_ref[...] = table[...].reshape(KEPT, KEPT)
-
-    @pl.when(is_owner)
-    def _():
-        for step in range(1, SQUARES):
-            other, copy = across(step)
-            pl.when(other)(copy.wait_send)
-        for turn in range(GROUP):
-            other, copy = to_mate(turn)
-            pl.when(other)(copy.wait_send)
 
     @pl.when(jnp.logical_and(is_far, is_owner))
     def _():
@@ -390,7 +391,7 @@
             dma((SQUARES, OWNERS)),
             dma((GROUP,)),
             dma((OWNERS,)),
-            pltpu.SemaphoreType.REGULAR((2, 4)),
+            pltpu.SemaphoreType.REGULAR((2, 3)),
         ],
         compiler_params=pltpu.CompilerParams(
             collective_id=0, has_side_effects=True, vmem_limit_bytes=24 * 2**20

time: 47.9 us -> 47.9 us (level)
  no operation moved by 1% of the time
where the time goes in v2:
time: 47.9 us; the launch traced here: 47.4 us
  Pallas kernels  47.4 us (99%)
    pallas_call x1, Pallas kernels, per_device(): pl.pallas_call(step_kernel, out_shape=(pltpu.VMEM((KEPT, KEPT), F32), plt...  45.5 us
    pallas_call x1, Pallas kernels, per_device(): pl.pallas_call(expand_kernel, out_shape=jax.ShapeDtypeStruct((ROWS, COLS)...  1.92 us

profile of v2, /device:TPU:1, one launch (start us, length us, event | category | flops | bytes accessed | tf_op | source)
XLA Modules:
  0.0 47.4 jit_solution(5778096961482341737)
XLA Ops:
  0.0 0.0 copy-start
  0.0 45.5 %step.1 = (f32[128,128]{1,0:T(8,128)S(1)}, bf16[256,1024]{1,0:T(8,128)(2,1)S(1)}) custom-call(bf16[512,1024]{1,0:T(8,128)(2,1)} %acts_hbm.1, bf16[64,1024]{1,0:T(8,128)(2,1)} %grad_hbm.1, bf16[1,1024,1024]{2,1,0:T(8,128)(2,1)} %moment_hbm.1, f32[128,1024]{1,0:T(8,128)} %constant.6.clone.wide_hbm, f32[1024,128]{1,0:T(8,128)} %constant.7.clone.tall_hbm), custom_call_target="tpu_custom_call" | custom-call | tf_op jit(solution)/shard_map/step/pallas_call | solution.py:365
  45.5 0.0 copy-done
  45.5 1.9 %expand.1 = bf16[1024,1024]{1,0:T(8,128)(2,1)} custom-call(f32[128,128]{1,0:T(8,128)S(1)} %get-tuple-element.7.summed_ref, bf16[256,1024]{1,0:T(8,128)(2,1)S(1)} %get-tuple-element.8.wide, f32[256,96]{1,0:T(8,128)S(1)} %copy-done), custom_call_target="tpu_custom_call" | custom-call | tf_op jit(solution)/shard_map/expand/pallas_call | solution.py:401
Async XLA Ops:
  0.0 45.5 %copy-start = (f32[256,96]{1,0:T(8,128)S(1)}, f32[256,96]{1,0:T(8,128)}, u32[]{:S(2)}) copy-start(f32[256,96]{1,0:T(8,128)} %constant.8.clone.block_ref) | copy-start | bytes 294916

commit v3 on v2

--- a/solution.py
+++ b/solution.py
@@ -341,11 +341,11 @@
     half = two_parts(half, 0)
     square_basis = block_ref[...].astype(BF16)
     copies = []
-    for i in range(4):
-        high = half[32 * i : 32 * (i + 1)]
-        low = half[KEPT + 32 * i : KEPT + 32 * (i + 1)]
+    for i in range(8):
+        high = half[16 * i : 16 * (i + 1)]
+        low = half[KEPT + 16 * i : KEPT + 16 * (i + 1)]
         out[i] = dot(square_basis, jnp.concatenate([high, high, low], axis=0)).astype(BF16)
-        copy = pltpu.make_async_copy(out.at[i], out_hbm.at[pl.ds(256 * i, 256)], out_sem.at[i])
+        copy = pltpu.make_async_copy(out.at[i], out_hbm.at[pl.ds(128 * i, 128)], out_sem.at[i])
         copy.start()
         copies.append(copy)
     for copy in copies:
@@ -354,7 +354,7 @@
 
 def per_device(activations, output_gradient, momentum):
     wide = block_basis()
-    corner = wide[:32, :256].T
+    corner = wide[:16, :128].T
     high = corner.astype(ml_dtypes.bfloat16).astype(np.float32)
     block = np.concatenate([high, corner - high, high], axis=1)
     wide, tall, block = jnp.asarray(wide), jnp.asarray(wide.T.copy()), jnp.asarray(block)
@@ -403,7 +403,7 @@
         out_shape=jax.ShapeDtypeStruct((ROWS, COLS), BF16),
         in_specs=[in_vmem] * 3,
         out_specs=anywhere,
-        scratch_shapes=[pltpu.VMEM((4, 256, COLS), BF16), dma((4,))],
+        scratch_shapes=[pltpu.VMEM((8, 128, COLS), BF16), dma((8,))],
         compiler_params=pltpu.CompilerParams(vmem_limit_bytes=24 * 2**20),
         name="expand",
     )(summed, wide, block)

time: 47.9 us -> 47.9 us (level)
  no operation moved by 1% of the time
where the time goes in v3:
time: 47.9 us; the launch traced here: 47.4 us
  Pallas kernels  47.4 us (99%)
    pallas_call x1, Pallas kernels, per_device(): pl.pallas_call(step_kernel, out_shape=(pltpu.VMEM((KEPT, KEPT), F32), plt...  45.5 us
    pallas_call x1, Pallas kernels, per_device(): pl.pallas_call(expand_kernel, out_shape=jax.ShapeDtypeStruct((ROWS, COLS)...  1.87 us

profile of v3, /device:TPU:1, one launch (start us, length us, event | category | flops | bytes accessed | tf_op | source)
XLA Modules:
  0.0 47.4 jit_solution(4372979323641884332)
XLA Ops:
  0.0 0.0 copy-start
  0.0 45.5 %step.1 = (f32[128,128]{1,0:T(8,128)S(1)}, bf16[256,1024]{1,0:T(8,128)(2,1)S(1)}) custom-call(bf16[512,1024]{1,0:T(8,128)(2,1)} %acts_hbm.1, bf16[64,1024]{1,0:T(8,128)(2,1)} %grad_hbm.1, bf16[1,1024,1024]{2,1,0:T(8,128)(2,1)} %moment_hbm.1, f32[128,1024]{1,0:T(8,128)} %constant.6.clone.wide_hbm, f32[1024,128]{1,0:T(8,128)} %constant.7.clone.tall_hbm), custom_call_target="tpu_custom_call" | custom-call | tf_op jit(solution)/shard_map/step/pallas_call | solution.py:365
  45.5 0.0 copy-done
  45.5 1.9 %expand.1 = bf16[1024,1024]{1,0:T(8,128)(2,1)} custom-call(f32[128,128]{1,0:T(8,128)S(1)} %get-tuple-element.7.summed_ref, bf16[256,1024]{1,0:T(8,128)(2,1)S(1)} %get-tuple-element.8.wide, f32[128,48]{1,0:T(8,128)S(1)} %copy-done), custom_call_target="tpu_custom_call" | custom-call | tf_op jit(solution)/shard_map/expand/pallas_call | solution.py:401
Async XLA Ops:
  0.0 45.5 %copy-start = (f32[128,48]{1,0:T(8,128)S(1)}, f32[128,48]{1,0:T(8,128)}, u32[]{:S(2)}) copy-start(f32[128,48]{1,0:T(8,128)} %constant.8.clone.block_ref) | copy-start | bytes 73732
